TPU v7x, 32 devices: a whole 2x2x4 slice. The times are simulated.
32 devices in a mesh: dp: 8 (over z, y), tr: 2 (over core), tc: 2 (over x).
Axes of the slice: x: 2, y: 2, z: 4, core: 2. Of those that a mesh axis runs over, the one named last changes fastest.
Arguments:
- block_in: bfloat16 [4096, 896], P(('dp', 'tc'), 'tr'), may hold values from -6 to 6
- g_attn: float32 [896], P('tr'), may hold values from 0.5 to 1.5
- query_key_value_weight: bfloat16 [896, 1152], P('tr', 'tc'), may hold values from -0.1875 to 0.1875
- query_key_value_bias: float32 [1152], P('tc'), may hold values from -3 to 3, as said below
- output_weight: bfloat16 [896, 896], P('tr', 'tc'), may hold values from -0.75 to 0.75
- g_mlp: float32 [896], P('tr'), may hold values from 0.5 to 1.5
- w_gu: bfloat16 [2, 896, 4864], P(None, 'tr', 'tc'), may hold values from -0.1875 to 0.1875
- w_down: bfloat16 [896, 4864], P('tr', 'tc'), may hold values from -0.078125 to 0.078125
- dy: bfloat16 [4096, 896], P(('dp', 'tc'), 'tr'), may hold values from -6 to 6
Outputs:
- block_out: bfloat16 [4096, 896], P(('dp', 'tc'), 'tr')
- dx: float32 [4096, 896], P(('dp', 'tc'), 'tr')
- d_w_qkv: float32 [896, 1152], P('tr', ('tc', 'dp'))
- d_b_qkv: float32 [1152], P(('tc', 'dp'))
- d_w_o: float32 [896, 896], P('tr', ('tc', 'dp'))
- d_w_gu: float32 [2, 896, 4864], P(None, 'tr', ('tc', 'dp'))
- d_w_down: float32 [896, 4864], P('tr', ('tc', 'dp'))
- d_g_attn: float32 [896], P(('tr', 'dp'))
- d_g_mlp: float32 [896], P(('tr', 'dp'))
Inputs may be any that keep to these rules, and one draw needn't show every extreme that they name: `query_key_value_bias`: biases of the query, key and value columns.
All inputs are finite; a program needn't handle non-finite values.
Results may differ from a plain program's by a relative error of at most 0.012.
Values may be sent and summed in bfloat16 or wider, within the bound.
A program may use at most 128 MiB of HBM per device.

v0:
```python
import jax
import jax.numpy as jnp
from jax import lax
from jax.sharding import PartitionSpec as P

QUERY_HEADS = 14
KEY_VALUE_HEADS = 2
HEAD_SIZE = 64
SEQUENCE_TOKENS = 512


EPS = 1e-06
ROPE_BASE = 1000000.0


def rotate_half(value):
    half = value.shape[-1] // 2
    return jnp.concatenate([-value[..., half:], value[..., :half]], axis=-1)


def rope_tables(positions, head_index):
    half = head_index // 2
    inverse = ROPE_BASE ** (-jnp.arange(half, dtype=jnp.float32) * 2.0 / head_index)
    angle = positions.astype(jnp.float32)[:, None] * inverse[None, :]
    angle = jnp.concatenate([angle, angle], axis=1)
    return (jnp.cos(angle), jnp.sin(angle))


def rope_apply(value, cosv, sinv):
    return value * cosv + rotate_half(value) * sinv


def rope_back(value, cosv, sinv):
    return value * cosv - rotate_half(value * sinv)


def contract_last(left, right):
    return lax.dot_general(
        left, right, (((1,), (1,)), ((), ())), preferred_element_type=jnp.float32
    )


def contract_first(left, right):
    return lax.dot_general(
        left, right, (((0,), (0,)), ((), ())), preferred_element_type=jnp.float32
    )


def row_total(values):
    return lax.psum(values, "tr")


def width_rows(values):
    return lax.all_gather(values, "tc", axis=0, tiled=True)


def width_sums(term, rows):
    return lax.psum_scatter(
        term(jnp.int32(0), lax.axis_size("tc") * rows), "tc", scatter_dimension=0, tiled=True
    )


def pair_rows(values):
    return lax.all_gather(values, "tr", axis=0, tiled=True)


def pair_sums(term, rows):
    return lax.psum_scatter(
        term(jnp.int32(0), lax.axis_size("tr") * rows), "tr", scatter_dimension=0, tiled=True
    )


def attend(query, keys, values, qpos, kpos):
    scale = query.shape[-1] ** (-0.5)
    scores = jnp.einsum("tkgd,skd->kgts", query, keys, preferred_element_type=jnp.float32) * scale
    scores = jnp.where(qpos[:, None] >= kpos[None, :], scores, -1e30)
    top = jnp.max(scores, axis=3, keepdims=True)
    lse = top + jnp.log(jnp.sum(jnp.exp(scores - top), axis=3, keepdims=True))
    prob = jnp.exp(scores - lse).astype(jnp.bfloat16)
    output = jnp.einsum("kgts,skd->tkgd", prob, values, preferred_element_type=jnp.float32).astype(
        jnp.bfloat16
    )
    return (output, lse)


def attend_back(query, keys, values, output, dout, lse, qpos, kpos):
    scale = query.shape[-1] ** (-0.5)
    scores = jnp.einsum("tkgd,skd->kgts", query, keys, preferred_element_type=jnp.float32) * scale
    scores = jnp.where(qpos[:, None] >= kpos[None, :], scores, -1e30)
    prob = jnp.exp(scores - lse)
    prob_b = prob.astype(jnp.bfloat16)
    delta = jnp.transpose(
        jnp.sum(dout.astype(jnp.float32) * output.astype(jnp.float32), axis=3), (1, 2, 0)
    )[..., None]
    dprob = jnp.einsum("tkgd,skd->kgts", dout, values, preferred_element_type=jnp.float32)
    dscore = (prob * (dprob - delta) * scale).astype(jnp.bfloat16)
    dquery = jnp.einsum("kgts,skd->tkgd", dscore, keys, preferred_element_type=jnp.float32)
    dkeys = jnp.einsum("kgts,tkgd->skd", dscore, query, preferred_element_type=jnp.float32)
    dvalues = jnp.einsum("kgts,tkgd->skd", prob_b, dout, preferred_element_type=jnp.float32)
    return (dquery, dkeys, dvalues)


def per_device(
    block_in,
    g_attn,
    query_key_value_weight,
    query_key_value_bias,
    output_weight,
    g_mlp,
    w_gu,
    w_down,
    dy,
):
    single_float_type = jnp.float32
    bfloat_type = jnp.bfloat16
    rows = block_in.shape[0]
    model_width = block_in.shape[1] * lax.axis_size("tr")
    head_group = QUERY_HEADS // KEY_VALUE_HEADS
    heads_kv = query_key_value_weight.shape[1] // ((head_group + 2) * HEAD_SIZE)
    block = rows * lax.axis_size("tc")
    xf = block_in.astype(single_float_type)
    r1 = lax.rsqrt(row_total(jnp.sum(xf * xf, axis=1)) / model_width + EPS)[:, None]
    first_normed_input = (xf * r1 * g_attn).astype(bfloat_type)
    xn1_all = width_rows(first_normed_input)

    def qkv_forward(start, count):
        return jnp.dot(xn1_all, query_key_value_weight, preferred_element_type=single_float_type)

    query_key_value = pair_sums(qkv_forward, rows) + query_key_value_bias
    query_key_value = query_key_value.reshape(rows, heads_kv, head_group + 2, HEAD_SIZE)
    first = lax.axis_index("tr") * rows
    cosv, sinv = rope_tables((first + jnp.arange(rows)) % SEQUENCE_TOKENS, HEAD_SIZE)
    query = rope_apply(
        query_key_value[:, :, :head_group], cosv[:, None, None], sinv[:, None, None]
    ).astype(bfloat_type)
    keys = rope_apply(query_key_value[:, :, head_group], cosv[:, None], sinv[:, None]).astype(
        bfloat_type
    )
    values = query_key_value[:, :, head_group + 1].astype(bfloat_type)
    kv_here = jnp.stack([keys, values], axis=2).reshape(rows, heads_kv * 2 * HEAD_SIZE)
    kv_all = pair_rows(kv_here).reshape(block, heads_kv, 2, HEAD_SIZE)
    seqs = max(rows // SEQUENCE_TOKENS, 1)
    qlen = min(rows, SEQUENCE_TOKENS)
    q_own = query.reshape(seqs, qlen, heads_kv, head_group, HEAD_SIZE)
    k_own = kv_all[:, :, 0].reshape(seqs, SEQUENCE_TOKENS, heads_kv, HEAD_SIZE)
    v_own = kv_all[:, :, 1].reshape(seqs, SEQUENCE_TOKENS, heads_kv, HEAD_SIZE)
    qpos = first + jnp.arange(qlen)
    kpos = jnp.arange(SEQUENCE_TOKENS)

    def forward_one(pieces):
        return attend(pieces[0], pieces[1], pieces[2], qpos, kpos)

    o_own, lse = lax.map(forward_one, (q_own, k_own, v_own))
    o_all = pair_rows(o_own.reshape(rows, heads_kv * head_group * HEAD_SIZE))

    def attn_term(start, count):
        return contract_last(o_all, output_weight)

    h1 = xf + width_sums(attn_term, rows)
    r2 = lax.rsqrt(row_total(jnp.sum(h1 * h1, axis=1)) / model_width + EPS)[:, None]
    xn2 = (h1 * r2 * g_mlp).astype(bfloat_type)
    xn2_all = width_rows(xn2)

    def gate_term(start, count):
        return jnp.einsum("td,gdf->tgf", xn2_all, w_gu, preferred_element_type=single_float_type)

    gate_up = pair_sums(gate_term, rows)
    gate = gate_up[:, 0]
    upper = gate_up[:, 1]
    sig = jax.nn.sigmoid(gate)
    silu_v = gate * sig
    mixed = (silu_v * upper).astype(bfloat_type)
    mixed_all = pair_rows(mixed)

    def down_term(start, count):
        return contract_last(mixed_all, w_down)

    block_out = (h1 + width_sums(down_term, rows)).astype(bfloat_type)
    dyf = dy.astype(single_float_type)
    dy_all = width_rows(dy)
    d_w_down = contract_first(dy_all, mixed_all)

    def hidden_term(start, count):
        return jnp.dot(dy_all, w_down, preferred_element_type=single_float_type)

    dmixed = pair_sums(hidden_term, rows)
    dgate = dmixed * upper * sig * (1.0 + gate * (1.0 - sig))
    dup = dmixed * silu_v
    dgu = jnp.stack([dgate, dup], axis=1).astype(bfloat_type)
    dgu_all = pair_rows(dgu)
    d_w_gu = jnp.einsum("td,tgf->gdf", xn2_all, dgu_all, preferred_element_type=single_float_type)

    def input_term(start, count):
        return jnp.einsum("tgf,gdf->td", dgu_all, w_gu, preferred_element_type=single_float_type)

    dxn2 = width_sums(input_term, rows)
    d_g_mlp = jnp.sum(dxn2 * h1 * r2, axis=0)
    scaled = g_mlp * dxn2
    dh1 = (
        dyf
        + r2 * scaled
        - h1 * r2**3 * row_total(jnp.sum(scaled * h1, axis=1))[:, None] / model_width
    )
    hidden_gradient_block = dh1.astype(bfloat_type)
    dh1_all = width_rows(hidden_gradient_block)
    d_w_o = contract_first(dh1_all, o_all)

    def head_term(start, count):
        return jnp.dot(dh1_all, output_weight, preferred_element_type=single_float_type)

    dout = pair_sums(head_term, rows).astype(bfloat_type)
    dout = dout.reshape(seqs, qlen, heads_kv, head_group, HEAD_SIZE)

    def backward_one(pieces):
        return attend_back(
            pieces[0], pieces[1], pieces[2], pieces[3], pieces[4], pieces[5], qpos, kpos
        )

    dquery, dkeys, dvalues = lax.map(backward_one, (q_own, k_own, v_own, o_own, dout, lse))
    kv_grad = jnp.stack([dkeys, dvalues], axis=3).reshape(
        seqs * SEQUENCE_TOKENS, heads_kv, 2, HEAD_SIZE
    )
    kv_part = kv_grad
    kv_part = kv_part.reshape(block, heads_kv * 2 * HEAD_SIZE)

    def kv_term(start, count):
        return kv_part

    kv_back = pair_sums(kv_term, rows).reshape(rows, heads_kv, 2, HEAD_SIZE)
    q_back = rope_back(
        dquery.reshape(rows, heads_kv, head_group, HEAD_SIZE),
        cosv[:, None, None],
        sinv[:, None, None],
    )
    k_back = rope_back(kv_back[:, :, 0], cosv[:, None], sinv[:, None])
    dqkv = jnp.concatenate(
        [q_back, k_back[:, :, None], kv_back[:, :, 1][:, :, None]], axis=2
    ).reshape(rows, -1)
    bias_part = jnp.sum(dqkv, axis=0)
    dqkv_all = pair_rows(dqkv.astype(bfloat_type))
    d_w_qkv = contract_first(xn1_all, dqkv_all)

    def qkv_term(start, count):
        return contract_last(dqkv_all, query_key_value_weight)

    dxn1 = width_sums(qkv_term, rows)
    d_g_attn = jnp.sum(dxn1 * xf * r1, axis=0)
    scaled = g_attn * dxn1
    stats = row_total((jnp.sum(scaled * xf, axis=1), bias_part))
    d_b_qkv = stats[1]
    dx = dh1 + r1 * scaled - xf * r1**3 * stats[0][:, None] / model_width
    gains = lax.psum((d_g_attn, d_g_mlp), "tc")
    grads = (
        lax.psum_scatter(d_w_qkv, "dp", scatter_dimension=1, tiled=True),
        lax.psum_scatter(d_b_qkv, "dp", scatter_dimension=0, tiled=True),
        lax.psum_scatter(d_w_o, "dp", scatter_dimension=1, tiled=True),
        lax.psum_scatter(d_w_gu, "dp", scatter_dimension=2, tiled=True),
        lax.psum_scatter(d_w_down, "dp", scatter_dimension=1, tiled=True),
        lax.psum_scatter(gains[0], "dp", scatter_dimension=0, tiled=True),
        lax.psum_scatter(gains[1], "dp", scatter_dimension=0, tiled=True),
    )
    return (block_out, dx, grads[0], grads[1], grads[2], grads[3], grads[4], grads[5], grads[6])


def solution(mesh):
    placed = (
        P(("dp", "tc"), "tr"),
        P("tr"),
        P("tr", "tc"),
        P("tc"),
        P("tr", "tc"),
        P("tr"),
        P(None, "tr", "tc"),
        P("tr", "tc"),
        P(("dp", "tc"), "tr"),
    )
    return jax.shard_map(
        per_device,
        mesh=mesh,
        in_specs=placed,
        out_specs=(
            P(("dp", "tc"), "tr"),
            P(("dp", "tc"), "tr"),
            P("tr", ("tc", "dp")),
            P(("tc", "dp")),
            P("tr", ("tc", "dp")),
            P(None, "tr", ("tc", "dp")),
            P("tr", ("tc", "dp")),
            P(("tr", "dp")),
            P(("tr", "dp")),
        ),
        check_vma=False,
    )
```

profile of v0, /device:TPU:0, one launch (start us, length us, event | category | flops | bytes accessed | tf_op | source)
XLA Modules:
  0.0 822.9 jit_solution(7265393819046371343)
XLA Ops:
  7.2 1.2 fusion.19
  8.4 2.6 psum.49
  12.1 1.1 fusion.21
  13.1 9.4 %all_gather.27 = bf16[512,448]{0,1:T(8,128)(2,1)S(1)} all-gather(bf16[256,448]{0,1:T(8,128)(2,1)S(1)} %fusion.21), channel_id=1, replica_groups=mesh['dp'=8,'tr'=2,'tc'=2] {'tc'}, dimensions={0}, use_global_device_ids=true | all-gather | bytes 688128 | tf_op jit(solution)/shard_map/all_gather | solution.py:54
  22.6 2.8 fusion.56
  26.4 9.3 %reduce-scatter.15.cloned.1.call-done = f32[256,576]{0,1:T(8,128)} async-done(((f32[512,576]{0,1:T(8,128)}), f32[256,576]{0,1:T(8,128)}) %reduce-scatter.15.cloned.1.call-update) | async-done | bytes 589840 | tf_op jit(solution)/shard_map/reduce_scatter | solution.py:68
  35.7 1.2 broadcast_add_fusion
  37.1 1.9 all_gather.28
  39.9 0.8 exponential_reduce_fusion
  40.7 1.0 convolution_convert_fusion
  42.5 2.1 all_gather.29
  44.6 1.3 fusion.62
  46.0 8.9 %all_gather.32 = bf16[512,448]{0,1:T(8,128)(2,1)S(1)} all-gather(bf16[256,448]{0,1:T(8,128)(2,1)S(1)} %copy-done.11), channel_id=1, replica_groups=mesh['dp'=8,'tr'=2,'tc'=2] {'tc'}, dimensions={0}, use_global_device_ids=true | all-gather | bytes 688128 | tf_op jit(solution)/shard_map/all_gather | solution.py:54
  54.9 3.9 fusion.58
  58.8 7.3 reduce-scatter.17.cloned.1.call-done
  66.1 1.7 multiply_reduce_fusion.2
  67.8 3.1 psum.50
  71.0 1.2 multiply_multiply_fusion.1
  72.7 0.8 multiply_convert_fusion.3
  73.5 8.4 %all_gather.30 = bf16[512,448]{0,1:T(8,128)(2,1)S(1)} all-gather(bf16[256,448]{0,1:T(8,128)(2,1)S(1)} %multiply_convert_fusion.3), channel_id=1, replica_groups=mesh['dp'=8,'tr'=2,'tc'=2] {'tc'}, dimensions={0}, use_global_device_ids=true | all-gather | bytes 688128 | tf_op jit(solution)/shard_map/all_gather | solution.py:54
  82.6 7.5 fusion.32
  90.3 18.9 %reduce-scatter.19.cloned.1.call-done = f32[256,2,2432]{2,0,1:T(8,128)} async-done(((f32[512,2,2432]{2,0,1:T(8,128)}), f32[256,2,2432]{2,0,1:T(8,128)}) %reduce-scatter.19.cloned.1.call-update) | async-done | bytes 4980752 | tf_op jit(solution)/shard_map/reduce_scatter | solution.py:68
  109.2 5.7 fusion.12
  114.9 1.7 pad_maximum_fusion
  116.7 16.2 %all-gather.5.cloned.1.call-done = bf16[512,2,2432]{2,0,1:T(8,128)(2,1)} async-done(((bf16[256,2,2432]{2,0,1:T(8,128)(2,1)}), bf16[512,2,2432]{2,0,1:T(8,128)(2,1)}) %all-gather.5.cloned.1.call-update) | async-done | bytes 4980752 | tf_op jit(solution)/shard_map/all_gather | solution.py:64
  132.8 7.1 convolution_bitcast_fusion.2
  140.0 20.1 %reduce-scatter.25.cloned.1.call-done = f32[256,448]{0,1:T(8,128)} async-done(((f32[512,448]{0,1:T(8,128)}), f32[256,448]{0,1:T(8,128)}) %reduce-scatter.25.cloned.1.call-update) | async-done | bytes 458768 | tf_op jit(solution)/shard_map/reduce_scatter | solution.py:58
  160.2 1.8 multiply_reduce_fusion
  162.0 3.1 psum.51
  165.1 1.2 fusion.55
  166.3 8.5 %all_gather.34 = bf16[512,448]{0,1:T(8,128)(2,1)S(1)} all-gather(bf16[256,448]{0,1:T(8,128)(2,1)S(1)} %fusion.55), channel_id=1, replica_groups=mesh['dp'=8,'tr'=2,'tc'=2] {'tc'}, dimensions={0}, use_global_device_ids=true | all-gather | bytes 688128 | tf_op jit(solution)/shard_map/all_gather | solution.py:54
  175.6 2.4 fusion.59
  178.1 8.5 %reduce-scatter.27.cloned.1.call-done = f32[256,448]{0,1:T(8,128)} async-done(((f32[512,448]{0,1:T(8,128)}), f32[256,448]{0,1:T(8,128)}) %reduce-scatter.27.cloned.1.call-update) | async-done | bytes 458768 | tf_op jit(solution)/shard_map/reduce_scatter | solution.py:68
  186.7 1.2 convert_element_type.106
  187.9 3.1 convolution_bitcast_fusion.3
  191.1 1.3 fusion.2
  192.4 1.3 copy-done.3
  196.0 1.9 broadcast_multiply_fusion
  198.1 6.1 reduce-scatter.29.cloned.1.call-done
  204.2 1.0 fusion.47
  205.2 1.0 fusion.43
  206.8 2.2 all_gather.35
  209.0 2.5 fusion.63
  211.6 7.0 all-gather.3.cloned.1.call-done
  218.6 4.0 fusion.57
  222.7 8.4 %convolution_bitcast_fusion = f32[2,448,2432]{2,1,0:T(8,128)} fusion(bf16[512,2,2432]{2,0,1:T(8,128)(2,1)} %all-gather.5.cloned.1.call-done, bf16[512,448]{0,1:T(8,128)(2,1)} %copy-done.6), kind=kOutput, calls=%fused_computation | convolution fusion | flops 2231369728 | bytes 14155776 | tf_op jit(solution)/shard_map/td,tgf->gdf/dot_general | solution.py:191
  231.1 15.2 %copy.28 = f32[2,448,2432]{1,0,2:T(2,128)} copy(f32[2,448,2432]{2,1,0:T(8,128)} %convolution_bitcast_fusion) | data formatting | bytes 17432576 | tf_op jit(solution)/shard_map/td,tgf->gdf/transpose | solution.py:191
  246.4 2.6 fusion.61
  249.1 5.4 convolution_bitcast_fusion.1
  254.5 5.6 copy.35
  260.2 2.6 fusion.60
  262.9 1.2 dynamic-slice.3
  266.1 1.2 fusion.34
  267.4 1.3 fusion.27
  268.6 22.8 %all-reduce.4 = (f32[576]{0:T(1024)S(1)}, f32[448]{0:T(512)S(1)}, f32[448]{0:T(512)S(1)}) all-reduce(f32[576]{0:T(1024)S(1)} %reduce_sum.95, f32[448]{0:T(512)S(1)} %get-tuple-element.89, f32[448]{0:T(512)S(1)} %copy-done.30), channel_id=12, replica_groups=mesh['dp'=8,'tr'=2,'tc'=2] {'dp'}, use_global_device_ids=true, to_apply=%region_23.24.clone | all-reduce | flops 1472 | bytes 11776
  291.7 5.4 all-reduce.5
  297.1 2.9 all-reduce.6
  300.1 2.5 fusion.24
  302.6 277.6 %all-reduce.9.cloned.1.call-done = f32[2,448,2432]{1,0,2:T(2,128)} async-done(((f32[2,448,2432]{1,0,2:T(2,128)}), f32[2,448,2432]{1,0,2:T(2,128)}) %all-reduce.9.cloned.1.call-update) | async-done | bytes 8716304
  580.2 1.7 constant_dynamic-slice_fusion
  581.9 1.3 copy.29
  583.2 62.9 %reduce-scatter.35.cloned.1.call-done = f32[448,56]{0,1:T(8,128)} async-done(((f32[448,448]{0,1:T(8,128)}), f32[448,56]{0,1:T(8,128)}) %reduce-scatter.35.cloned.1.call-update) | async-done | bytes 100368 | tf_op jit(solution)/shard_map/reduce_scatter | solution.py:256
  646.1 102.6 %reduce-scatter.37.cloned.1.call-done = f32[304,448]{1,0:T(8,128)} async-done(((f32[2432,448]{1,0:T(8,128)}), f32[304,448]{1,0:T(8,128)}) %reduce-scatter.37.cloned.1.call-update) | async-done | bytes 544784
  748.8 67.6 %reduce-scatter.33.cloned.1.call-done = f32[448,72]{0,1:T(8,128)} async-done(((f32[448,576]{0,1:T(8,128)}), f32[448,72]{0,1:T(8,128)}) %reduce-scatter.33.cloned.1.call-update) | async-done | bytes 129040 | tf_op jit(solution)/shard_map/reduce_scatter | solution.py:254
  (129 shorter events, 9.9 us)
Async XLA Ops:
  7.2 47.7 %copy-start = (bf16[448,2432]{1,0:T(8,128)(2,1)S(1)}, bf16[448,2432]{1,0:T(8,128)(2,1)}, u32[]{:S(2)}) copy-start(bf16[448,2432]{1,0:T(8,128)(2,1)} %param.16) | copy-start | bytes 6537220
  7.2 28.5 %copy-start.34 = (f32[576]{0:T(1024)S(1)}, f32[576]{0:T(1024)}, u32[]{:S(2)}) copy-start(f32[576]{0:T(1024)} %param.12) | copy-start | bytes 6916
  7.2 28.5 %reduce-scatter.15.cloned.1.call-start = ((), (), s32[]{:S(2)}) async-start(), calls=%async_computation.12 | async-start | bytes 1769472 | tf_op jit(solution)/shard_map/reduce_scatter | solution.py:68
  11.5 0.5 copy-start.26
  22.6 16.6 %copy-start.10 = (bf16[512,448]{0,1:T(8,128)(2,1)}, bf16[512,448]{0,1:T(8,128)(2,1)S(1)}, u32[]{:S(2)}) copy-start(bf16[512,448]{0,1:T(8,128)(2,1)S(1)} %all_gather.27) | copy-start | bytes 1376260
  25.3 40.8 %reduce-scatter.17.cloned.1.call-start = ((), (), s32[]{:S(2)}) async-start(), calls=%async_computation.13 | async-start | bytes 1376256 | tf_op jit(solution)/shard_map/reduce_scatter | solution.py:58
  26.2 13.6 %copy-start.15 = (f32[256,64]{0,1:T(8,128)}, f32[256,64]{0,1:T(8,128)S(1)}, u32[]{:S(2)}) copy-start(f32[256,64]{0,1:T(8,128)S(1)} %get-tuple-element.116) | copy-start | bytes 196612
  39.0 1.7 copy-start.18
  39.9 1.9 copy-start.1
  40.7 3.9 copy-start.12
  40.7 5.2 copy-start.31
  40.7 5.3 copy-start.11
  41.8 0.7 copy-start.13
  44.6 1.4 copy-start.7
  45.9 44.3 %reduce-scatter.23.cloned.1.call-start = ((), (), s32[]{:S(2)}) async-start(), calls=%async_computation.17 | async-start | bytes 7471104 | tf_op jit(solution)/shard_map/reduce_scatter | solution.py:68
  54.9 3.9 copy-start.5
  58.8 7.4 copy-start.4
  58.8 50.4 %reduce-scatter.19.cloned.1.call-start = ((), (), s32[]{:S(2)}) async-start(), calls=%async_computation.14 | async-start | bytes 14942208 | tf_op jit(solution)/shard_map/reduce_scatter | solution.py:68
  72.2 0.5 copy-start.23
  81.8 0.8 copy-start.6
  90.2 42.6 %all-gather.5.cloned.1.call-start = ((), (), s32[]{:S(2)}) async-start(), calls=%async_computation.18 | async-start | bytes 7471104 | tf_op jit(solution)/shard_map/all_gather | solution.py:64
  116.6 43.6 %reduce-scatter.25.cloned.1.call-start = ((), (), s32[]{:S(2)}) async-start(), calls=%async_computation.19 | async-start | bytes 1376256 | tf_op jit(solution)/shard_map/reduce_scatter | solution.py:58
  140.0 46.7 %reduce-scatter.27.cloned.1.call-start = ((), (), s32[]{:S(2)}) async-start(), calls=%async_computation.20 | async-start | bytes 1376256 | tf_op jit(solution)/shard_map/reduce_scatter | solution.py:68
  174.8 0.8 copy-start.8
  178.1 12.9 %copy-start.14 = (bf16[64,7,256]{2,0,1:T(8,128)(2,1)S(1)}, bf16[64,7,256]{2,0,1:T(8,128)(2,1)}, u32[]{:S(2)}) copy-start(bf16[64,7,256]{2,0,1:T(8,128)(2,1)} %copy-done.13) | copy-start | bytes 688132
  178.1 26.1 %reduce-scatter.29.cloned.1.call-start = ((), (), s32[]{:S(2)}) async-start(), calls=%async_computation.21 | async-start | bytes 393216 | tf_op jit(solution)/shard_map/reduce_scatter | solution.py:68
  186.6 4.4 copy-start.2
  186.7 4.4 copy-start.19
  186.7 4.4 copy-start.32
  192.4 1.3 copy-start.3
  193.7 2.2 copy-start.16
  193.7 2.2 copy-start.20
  194.4 9.8 %copy-start.21 = (f32[256,1,32]{0,2,1:T(8,128)S(1)}, f32[256,1,32]{0,2,1:T(8,128)}, u32[]{:S(2)}) copy-start(f32[256,1,32]{0,2,1:T(8,128)} %get-tuple-element.117) | copy-start | bytes 98308
  195.2 23.5 %all-gather.3.cloned.1.call-start = ((), (), s32[]{:S(2)}) async-start(), calls=%async_computation.15 | async-start | bytes 3735552 | tf_op jit(solution)/shard_map/all_gather | solution.py:64
  195.9 71.4 %reduce-scatter.31.cloned.1.call-start = ((), (), s32[]{:S(2)}) async-start(), calls=%async_computation.22 | async-start | bytes 1376256 | tf_op jit(solution)/shard_map/reduce_scatter | solution.py:58
  198.0 8.2 copy-start.9
  206.2 0.6 copy-start.17
  211.5 88.6 %reduce-scatter.21.cloned.1.call-start = ((), (), s32[]{:S(2)}) async-start(), calls=%async_computation.16 | async-start | bytes 1376256 | tf_op jit(solution)/shard_map/reduce_scatter | solution.py:58
  222.7 357.5 %all-reduce.9.cloned.1.call-start = ((), (), s32[]{:S(2)}) async-start(), calls=%async_computation.26 | async-start | bytes 19922944
  246.4 399.8 %reduce-scatter.35.cloned.1.call-start = ((), (), s32[]{:S(2)}) async-start(), calls=%async_computation.24 | async-start | bytes 1032192 | tf_op jit(solution)/shard_map/reduce_scatter | solution.py:256
  249.0 499.7 %reduce-scatter.37.cloned.1.call-start = ((), (), s32[]{:S(2)}) async-start(), calls=%async_computation.25 | async-start | bytes 5603328
  260.1 7.3 copy-start.25
  260.1 7.3 copy-start.27
  260.1 8.5 %copy-start.30 = (f32[448]{0:T(512)S(1)}, f32[448]{0:T(512)}, u32[]{:S(2)}) copy-start(f32[448]{0:T(512)} %get-tuple-element.87) | copy-start | bytes 5380
  260.1 40.0 %copy-start.22 = (f32[448]{0:T(512)S(1)}, f32[448]{0:T(512)}, u32[]{:S(2)}) copy-start(f32[448]{0:T(512)} %param.14) | copy-start | bytes 5380
  260.1 40.0 %copy-start.24 = (f32[256]{0:T(256)S(1)}, f32[256]{0:T(256)}, u32[]{:S(2)}) copy-start(f32[256]{0:T(256)} %copy-done.23) | copy-start | bytes 3076
  260.1 40.0 %copy-start.28 = (f32[256]{0:T(256)S(1)}, f32[256]{0:T(256)}, u32[]{:S(2)}) copy-start(f32[256]{0:T(256)} %get-tuple-element.122) | copy-start | bytes 3076
  260.1 40.0 %copy-start.29 = (f32[256]{0:T(256)S(1)}, f32[256]{0:T(256)}, u32[]{:S(2)}) copy-start(f32[256]{0:T(256)} %psum.51) | copy-start | bytes 3076
  260.1 40.0 %copy-start.33 = (f32[256]{0:T(256)S(1)}, f32[256]{0:T(256)}, u32[]{:S(2)}) copy-start(f32[256]{0:T(256)} %get-tuple-element.120) | copy-start | bytes 3076
  260.2 556.2 %reduce-scatter.33.cloned.1.call-start = ((), (), s32[]{:S(2)}) async-start(), calls=%async_computation.23 | async-start | bytes 1327104 | tf_op jit(solution)/shard_map/reduce_scatter | solution.py:254
Sparse Core Ops, SparseCore 0:
  25.4 10.1 reduce-scatter.14
  46.0 20.0 reduce-scatter.16
  68.4 13.3 reduce-scatter.22
  90.3 18.8 reduce-scatter.18
  116.7 16.0 all-gather.4
  140.1 20.0 reduce-scatter.24
  178.2 8.4 reduce-scatter.26
  195.3 8.8 reduce-scatter.28
  206.3 12.2 all-gather.2
  220.7 20.0 reduce-scatter.30
  243.7 18.8 reduce-scatter.20
  266.4 313.8 all-reduce.8
  584.1 61.9 reduce-scatter.34
  650.7 98.0 reduce-scatter.36
  752.6 63.7 reduce-scatter.32
where the time goes:
time: 824 us; the launch traced here: 823 us
  waiting for transfers between devices  605 us (73%)
  blocking collectives  81.4 us (10%)
  matrix products  59.4 us (7%)
  local copies, waits for them, and re-layouts  30.6 us (4%)
  other arithmetic  29.2 us (4%)
  between operations  16.4 us (2%)
    unnamed x17, waiting for transfers between devices  381 us
    reduce_scatter x1, waiting for transfers between devices, per_device(): lax.psum_scatter(d_w_qkv, 'dp', scatter_dimension=1, tiled=True)  67.6 us
    reduce_scatter x1, waiting for transfers between devices, per_device(): lax.psum_scatter(d_w_o, 'dp', scatter_dimension=1, tiled=True)  62.9 us
    reduce_scatter x5, waiting for transfers between devices, pair_sums(): lax.psum_scatter(term(jnp.int32(0), lax.axis_size('tr') * rows), 'tr', sc...  42.9 us
    all_gather x4, blocking collectives, width_rows(): return lax.all_gather(values, 'tc', axis=0, tiled=True)  35.2 us
    reduce_scatter x4, waiting for transfers between devices, width_sums(): lax.psum_scatter(term(jnp.int32(0), lax.axis_size('tc') * rows), 'tc', sc...  27.4 us
    all_gather x2, waiting for transfers between devices, pair_rows(): return lax.all_gather(values, 'tr', axis=0, tiled=True)  23.2 us
    unnamed x1, blocking collectives  22.8 us
  transfers between devices with their start and end apart: 15, of which 12 were waited for; matrix products, arithmetic and copies ran while one was open for 9% of the time, Pallas kernels for 0%

commit v1 on v0

--- a/solution.py
+++ b/solution.py
@@ -68,6 +68,39 @@
     return lax.psum_scatter(
         term(jnp.int32(0), lax.axis_size("tr") * rows), "tr", scatter_dimension=0, tiled=True
     )
+
+
+def swapped(values, axis, bit):
+    size = lax.axis_size(axis)
+    return lax.ppermute(values, axis, [(i, i ^ bit) for i in range(size)])
+
+
+def scatter_sum(grad, first):
+    size = lax.axis_size("dp")
+    bits = size.bit_length() - 1
+    me = lax.axis_index("dp")
+    lead = grad.shape[0]
+    value = grad.reshape((lead,) + (2,) * bits + (grad.shape[1] // size, grad.shape[2]))
+    order = list(range(bits))
+    if first == 1 and bits > 1:
+        order[0], order[1] = 1, 0
+    left = list(range(bits))[::-1]
+    for step, bit in enumerate(order):
+        dim = 1 + left.index(bit)
+        mine = lax.rem(me // (1 << bit), 2)
+        keep = lax.dynamic_index_in_dim(value, mine, dim, keepdims=False)
+        send = lax.dynamic_index_in_dim(value, 1 - mine, dim, keepdims=False)
+        got = swapped(send, "dp", 1 << bit)
+        value = keep.astype(jnp.float32) + got.astype(jnp.float32)
+        if step < bits - 1:
+            value = value.astype(jnp.bfloat16)
+        left.remove(bit)
+    return value
+
+
+def grad_block(left, right, first):
+    grad = contract_first(left, right).astype(jnp.bfloat16)
+    return scatter_sum(grad[None], first)[0].T
 
 
 def attend(query, keys, values, qpos, kpos):
@@ -178,7 +211,7 @@
     block_out = (h1 + width_sums(down_term, rows)).astype(bfloat_type)
     dyf = dy.astype(single_float_type)
     dy_all = width_rows(dy)
-    d_w_down = contract_first(dy_all, mixed_all)
+    d_w_down = grad_block(mixed_all, dy_all, 0)
 
     def hidden_term(start, count):
         return jnp.dot(dy_all, w_down, preferred_element_type=single_float_type)
@@ -188,7 +221,7 @@
     dup = dmixed * silu_v
     dgu = jnp.stack([dgate, dup], axis=1).astype(bfloat_type)
     dgu_all = pair_rows(dgu)
-    d_w_gu = jnp.einsum("td,tgf->gdf", xn2_all, dgu_all, preferred_element_type=single_float_type)
+    d_w_gu = jnp.stack([grad_block(dgu_all[:, 0], xn2_all, 1), grad_block(dgu_all[:, 1], xn2_all, 0)])
 
     def input_term(start, count):
         return jnp.einsum("tgf,gdf->td", dgu_all, w_gu, preferred_element_type=single_float_type)
@@ -203,7 +236,7 @@
     )
     hidden_gradient_block = dh1.astype(bfloat_type)
     dh1_all = width_rows(hidden_gradient_block)
-    d_w_o = contract_first(dh1_all, o_all)
+    d_w_o = grad_block(o_all, dh1_all, 1)
 
     def head_term(start, count):
         return jnp.dot(dh1_all, output_weight, preferred_element_type=single_float_type)
@@ -238,7 +271,7 @@
     ).reshape(rows, -1)
     bias_part = jnp.sum(dqkv, axis=0)
     dqkv_all = pair_rows(dqkv.astype(bfloat_type))
-    d_w_qkv = contract_first(xn1_all, dqkv_all)
+    d_w_qkv = grad_block(dqkv_all, xn1_all, 0)
 
     def qkv_term(start, count):
         return contract_last(dqkv_all, query_key_value_weight)
@@ -251,11 +284,11 @@
     dx = dh1 + r1 * scaled - xf * r1**3 * stats[0][:, None] / model_width
     gains = lax.psum((d_g_attn, d_g_mlp), "tc")
     grads = (
-        lax.psum_scatter(d_w_qkv, "dp", scatter_dimension=1, tiled=True),
+        d_w_qkv,
         lax.psum_scatter(d_b_qkv, "dp", scatter_dimension=0, tiled=True),
-        lax.psum_scatter(d_w_o, "dp", scatter_dimension=1, tiled=True),
-        lax.psum_scatter(d_w_gu, "dp", scatter_dimension=2, tiled=True),
-        lax.psum_scatter(d_w_down, "dp", scatter_dimension=1, tiled=True),
+        d_w_o,
+        d_w_gu,
+        d_w_down,
         lax.psum_scatter(gains[0], "dp", scatter_dimension=0, tiled=True),
         lax.psum_scatter(gains[1], "dp", scatter_dimension=0, tiled=True),
     )

time: 824 us -> 401 us (0.49)
  waiting for transfers between devices: 605 us -> 145 us
  starting transfers between devices: 0.62 us -> 21 us
  other arithmetic: 29.2 us -> 43.2 us
  local copies, waits for them, and re-layouts: 30.6 us -> 41.1 us
    unnamed x17 -> x11, waiting for transfers between devices: 381 us -> 0.86 us
    reduce_scatter x2 -> x0, waiting for transfers between devices: 131 us -> none  [the longest x1 67.6 us: per_device(): lax.psum_scatter(d_w_qkv, 'dp', scatter_dimension=1, tiled=True)]
    ppermute x0 -> x15, waiting for transfers between devices: none -> 69.2 us  [swapped(): return lax.ppermute(values, axis, [(i, i ^ bit) for i in range(size)])]
    ppermute x0 -> x15, starting transfers between devices: none -> 20.5 us  [swapped(): return lax.ppermute(values, axis, [(i, i ^ bit) for i in range(size)])]
    transpose x1 -> x0, local copies, waits for them, and re-layouts: 15.2 us -> none  [per_device(): jnp.einsum('td,tgf->gdf', xn2_all, dgu_all, preferred_element_type=single...]
    convert_element_type x0 -> x4, local copies, waits for them, and re-layouts: none -> 14.1 us  [grad_block(): grad = contract_first(left, right).astype(jnp.bfloat16)]
    reduce_scatter x5, waiting for transfers between devices: 42.9 us -> 33.2 us  [pair_sums(): lax.psum_scatter(term(jnp.int32(0), lax.axis_size('tr') * rows), 'tr', sc...]
    convert_element_type x0 -> x10, other arithmetic: none -> 9.58 us  [scatter_sum(): value = value.astype(jnp.bfloat16)]
  transfers between devices with their start and end apart: 15 -> 26, of which waited for: 12 -> 15; matrix products, arithmetic and copies ran while one was open for 9% -> 25% of each run, Pallas kernels for 0% -> 0%
where the time goes in v1:
time: 401 us; the launch traced here: 399 us
  waiting for transfers between devices  145 us (36%)
  blocking collectives  79.8 us (20%)
  matrix products  53.1 us (13%)
  other arithmetic  43.2 us (11%)
  local copies, waits for them, and re-layouts  41.1 us (10%)
  starting transfers between devices  21 us (5%)
  between operations  16 us (4%)
    ppermute x15, waiting for transfers between devices, swapped(): return lax.ppermute(values, axis, [(i, i ^ bit) for i in range(size)])  69.2 us
    all_gather x4, blocking collectives, width_rows(): return lax.all_gather(values, 'tc', axis=0, tiled=True)  35.2 us
    reduce_scatter x5, waiting for transfers between devices, pair_sums(): lax.psum_scatter(term(jnp.int32(0), lax.axis_size('tr') * rows), 'tr', sc...  33.2 us
    reduce_scatter x4, waiting for transfers between devices, width_sums(): lax.psum_scatter(term(jnp.int32(0), lax.axis_size('tc') * rows), 'tc', sc...  25.9 us
    unnamed x1, blocking collectives  20.8 us
    ppermute x15, starting transfers between devices, swapped(): return lax.ppermute(values, axis, [(i, i ^ bit) for i in range(size)])  20.5 us
    all_gather x2, waiting for transfers between devices, pair_rows(): return lax.all_gather(values, 'tr', axis=0, tiled=True)  16.2 us
    dot_general x5, matrix products, contract_first(): lax.dot_general(left, right, (((0,), (0,)), ((), ())), preferred_element_...  15.3 us
  transfers between devices with their start and end apart: 26, of which 15 were waited for; matrix products, arithmetic and copies ran while one was open for 25% of the time, Pallas kernels for 0%

profile of v1, /device:TPU:0, one launch (start us, length us, event | category | flops | bytes accessed | tf_op | source)
XLA Modules:
  0.0 399.5 jit_solution(11675913575974999124)
XLA Ops:
  8.4 2.6 psum.49
  13.2 9.4 %all_gather.27 = bf16[512,448]{0,1:T(8,128)(2,1)S(1)} all-gather(bf16[256,448]{0,1:T(8,128)(2,1)S(1)} %fusion.31), channel_id=1, replica_groups=mesh['dp'=8,'tr'=2,'tc'=2] {'tc'}, dimensions={0}, use_global_device_ids=true | all-gather | bytes 688128 | tf_op jit(solution)/shard_map/all_gather | solution.py:54
  22.7 2.8 fusion.70
  26.5 9.3 %reduce-scatter.10.cloned.1.call-done = f32[256,576]{0,1:T(8,128)} async-done(((f32[512,576]{0,1:T(8,128)}), f32[256,576]{0,1:T(8,128)}) %reduce-scatter.10.cloned.1.call-update) | async-done | bytes 589840 | tf_op jit(solution)/shard_map/reduce_scatter | solution.py:68
  37.2 1.9 all_gather.28
  42.5 2.1 all_gather.29
  46.1 8.9 %all_gather.32 = bf16[512,448]{0,1:T(8,128)(2,1)S(1)} all-gather(bf16[256,448]{0,1:T(8,128)(2,1)S(1)} %copy-done.19), channel_id=1, replica_groups=mesh['dp'=8,'tr'=2,'tc'=2] {'tc'}, dimensions={0}, use_global_device_ids=true | all-gather | bytes 688128 | tf_op jit(solution)/shard_map/all_gather | solution.py:54
  55.7 3.9 fusion.72
  59.7 6.5 %reduce-scatter.12.cloned.1.call-done = f32[256,448]{0,1:T(8,128)} async-done(((f32[512,448]{0,1:T(8,128)}), f32[256,448]{0,1:T(8,128)}) %reduce-scatter.12.cloned.1.call-update) | async-done | bytes 458768 | tf_op jit(solution)/shard_map/reduce_scatter | solution.py:58
  66.3 1.7 multiply_reduce_fusion.2
  67.9 3.1 psum.50
  73.7 8.4 %all_gather.30 = bf16[512,448]{0,1:T(8,128)(2,1)S(1)} all-gather(bf16[256,448]{0,1:T(8,128)(2,1)S(1)} %multiply_convert_fusion.3), channel_id=1, replica_groups=mesh['dp'=8,'tr'=2,'tc'=2] {'tc'}, dimensions={0}, use_global_device_ids=true | all-gather | bytes 688128 | tf_op jit(solution)/shard_map/all_gather | solution.py:54
  82.8 7.6 %fusion.42 = f32[512,2,2432]{2,0,1:T(8,128)} fusion(bf16[2,448,2432]{2,1,0:T(8,128)(2,1)} %param.15, bf16[512,448]{0,1:T(8,128)(2,1)S(1)} %all_gather.30), kind=kOutput, calls=%fused_computation.90 | convolution fusion | flops 2231369728 | bytes 14778368 | tf_op jit(solution)/shard_map/td,gdf->tgf/dot_general | solution.py:198
  90.6 19.0 %reduce-scatter.14.cloned.1.call-done = f32[256,2,2432]{2,0,1:T(8,128)} async-done(((f32[512,2,2432]{2,0,1:T(8,128)}), f32[256,2,2432]{2,0,1:T(8,128)}) %reduce-scatter.14.cloned.1.call-update) | async-done | bytes 4980752 | tf_op jit(solution)/shard_map/reduce_scatter | solution.py:68
  109.5 5.7 %fusion.18 = (bf16[256,1,2432]{2,0,1:T(8,128)(2,1)S(1)}, bf16[256,1,2432]{2,0,1:T(8,128)(2,1)S(1)}, bf16[256,2432]{1,0:T(8,128)(2,1)}) fusion(f32[256,2,2432]{2,0,1:T(8,128)} %reduce-scatter.14.cloned.1.call-done, f32[256,2432]{1,0:T(8,128)} %reduce-scatter.18.cloned.1.call-done), kind=kLoop, calls=%fused_computation.48 | loop fusion | flops 9338880 | bytes 11206656 | tf_op jit(solution)/shard_map/stack | solution.py:222
  115.2 1.7 pad_maximum_fusion
  116.9 16.1 %all-gather.5.cloned.1.call-done = bf16[512,2,2432]{2,0,1:T(8,128)(2,1)} async-done(((bf16[256,2,2432]{2,0,1:T(8,128)(2,1)}), bf16[512,2,2432]{2,0,1:T(8,128)(2,1)}) %all-gather.5.cloned.1.call-update) | async-done | bytes 4980752 | tf_op jit(solution)/shard_map/all_gather | solution.py:64
  133.1 7.2 %convolution_bitcast_fusion = f32[512,448]{0,1:T(8,128)} fusion(bf16[512,2,2432]{2,0,1:T(8,128)(2,1)} %all-gather.5.cloned.1.call-done, bf16[2,448,2432]{2,1,0:T(8,128)(2,1)} %param.15), kind=kOutput, calls=%fused_computation.33 | convolution fusion | flops 2231369728 | bytes 10256384 | tf_op jit(solution)/shard_map/tgf,gdf->td/dot_general | solution.py:227
  141.1 19.4 %reduce-scatter.20.cloned.1.call-done = f32[256,448]{0,1:T(8,128)} async-done(((f32[512,448]{0,1:T(8,128)}), f32[256,448]{0,1:T(8,128)}) %reduce-scatter.20.cloned.1.call-update) | async-done | bytes 458768 | tf_op jit(solution)/shard_map/reduce_scatter | solution.py:58
  160.5 1.8 multiply_reduce_fusion
  162.3 3.2 psum.51
  166.7 8.5 %all_gather.34 = bf16[512,448]{0,1:T(8,128)(2,1)S(1)} all-gather(bf16[256,448]{0,1:T(8,128)(2,1)S(1)} %fusion.69), channel_id=1, replica_groups=mesh['dp'=8,'tr'=2,'tc'=2] {'tc'}, dimensions={0}, use_global_device_ids=true | all-gather | bytes 688128 | tf_op jit(solution)/shard_map/all_gather | solution.py:54
  176.1 2.4 fusion.73
  180.6 4.6 %convolution_convert_fusion = bf16[2432,448]{0,1:T(8,128)(2,1)} fusion(bf16[512,448]{0,1:T(8,128)(2,1)} %copy-done.26, bf16[512,2432]{1,0:T(8,128)(2,1)} %all-gather.3.cloned.1.call-done), kind=kOutput, calls=%fused_computation | convolution fusion | flops 1116774400 | bytes 5128192 | tf_op jit(solution)/shard_map/dot_general | solution.py:44
  185.1 4.3 %copy.55 = bf16[2432,448]{1,0:T(8,128)(2,1)} copy(bf16[2432,448]{0,1:T(8,128)(2,1)} %convolution_convert_fusion) | data formatting | bytes 4358144 | tf_op jit(solution)/shard_map/convert_element_type | solution.py:102
  189.4 2.4 dynamic-slice_bitcast_fusion
  191.8 1.5 collective-permute-start.12
  194.4 3.2 convolution_bitcast_fusion.1
  201.8 1.9 broadcast_multiply_fusion
  203.8 4.9 %reduce-scatter.24.cloned.1.call-done = f32[256,128]{0,1:T(8,128)} async-done(((f32[512,128]{0,1:T(8,128)}), f32[256,128]{0,1:T(8,128)}) %reduce-scatter.24.cloned.1.call-update) | async-done | bytes 131088 | tf_op jit(solution)/shard_map/reduce_scatter | solution.py:68
  211.4 2.2 all_gather.35
  214.5 1.4 fusion.75
  216.0 4.8 %collective-permute-done.12 = bf16[1,2,2,304,448]{4,3,2,1,0:T(8,128)(2,1)} collective-permute-done((bf16[1,2,2,304,448]{4,3,2,1,0:T(8,128)(2,1)}, bf16[1,2,2,304,448]{4,3,2,1,0:T(8,128)(2,1)}, u32[]{:S(2)}, u32[]{:S(2)}) %collective-permute-start.12) | collective-permute-done | bytes 1089568 | tf_op jit(solution)/shard_map/ppermute | solution.py:75
  220.8 2.0 fusion.4
  224.8 1.5 collective-permute-start.13
  226.4 4.4 %convolution_convert_fusion.1 = bf16[2432,448]{0,1:T(8,128)(2,1)} fusion(bf16[512,448]{0,1:T(8,128)(2,1)S(1)} %copy-done.25, bf16[512,2,2432]{2,0,1:T(8,128)(2,1)} %all-gather.5.cloned.1.call-done), kind=kOutput, calls=%fused_computation.1 | convolution fusion | flops 1116774400 | bytes 5128192 | tf_op jit(solution)/shard_map/dot_general | solution.py:44
  230.8 4.3 %copy.52 = bf16[2432,448]{1,0:T(8,128)(2,1)} copy(bf16[2432,448]{0,1:T(8,128)(2,1)} %convolution_convert_fusion.1) | data formatting | bytes 4358144 | tf_op jit(solution)/shard_map/convert_element_type | solution.py:102
  235.1 3.0 constant_dynamic-slice_fusion.1
  239.2 1.5 collective-permute-start.9
  240.7 4.5 %convolution_convert_fusion.2 = bf16[2432,448]{0,1:T(8,128)(2,1)} fusion(bf16[512,448]{0,1:T(8,128)(2,1)S(1)} %copy-done.25, bf16[512,2,2432]{2,0,1:T(8,128)(2,1)} %all-gather.5.cloned.1.call-done), kind=kOutput, calls=%fused_computation.2 | convolution fusion | flops 1116774400 | bytes 5128192 | tf_op jit(solution)/shard_map/dot_general | solution.py:44
  245.2 4.3 %copy.51 = bf16[2432,448]{1,0:T(8,128)(2,1)} copy(bf16[2432,448]{0,1:T(8,128)(2,1)} %convolution_convert_fusion.2) | data formatting | bytes 4358144 | tf_op jit(solution)/shard_map/convert_element_type | solution.py:102
  249.4 2.6 dynamic-slice_bitcast_fusion.1
  252.5 2.3 fusion.71
  254.8 1.5 fusion.15
  256.4 2.5 collective-permute-start.14
  258.9 8.1 %collective-permute-done.9 = bf16[1,2,2,304,448]{4,3,1,2,0:T(8,128)(2,1)} collective-permute-done((bf16[1,2,2,304,448]{4,3,1,2,0:T(8,128)(2,1)}, bf16[1,2,2,304,448]{4,3,1,2,0:T(8,128)(2,1)}, u32[]{:S(2)}, u32[]{:S(2)}) %collective-permute-start.9) | collective-permute-done | bytes 1089568 | tf_op jit(solution)/shard_map/ppermute | solution.py:75
  267.0 1.8 fusion.5
  269.4 19.9 %collective-permute-done.6 = bf16[1,2,2,304,448]{4,3,2,1,0:T(8,128)(2,1)} collective-permute-done((bf16[1,2,2,304,448]{4,3,2,1,0:T(8,128)(2,1)}, bf16[1,2,2,304,448]{4,3,2,1,0:T(8,128)(2,1)}, u32[]{:S(2)}, u32[]{:S(2)}) %collective-permute-start.6) | collective-permute-done | bytes 1089568 | tf_op jit(solution)/shard_map/ppermute | solution.py:75
  289.3 1.6 fusion.6
  292.5 6.9 %collective-permute-done.10 = bf16[1,2,304,448]{3,2,1,0:T(8,128)(2,1)S(1)} collective-permute-done((bf16[1,2,304,448]{3,2,1,0:T(8,128)(2,1)S(1)}, bf16[1,2,304,448]{3,2,1,0:T(8,128)(2,1)S(1)}, u32[]{:S(2)}, u32[]{:S(2)}) %collective-permute-start.10) | collective-permute-done | bytes 544800 | tf_op jit(solution)/shard_map/ppermute | solution.py:75
  299.6 3.4 collective-permute-start.11
  306.3 15.1 %collective-permute-done.11 = bf16[1,304,448]{2,1,0:T(8,128)(2,1)S(1)} collective-permute-done((bf16[1,304,448]{2,1,0:T(8,128)(2,1)S(1)}, bf16[1,304,448]{2,1,0:T(8,128)(2,1)S(1)}, u32[]{:S(2)}, u32[]{:S(2)}) %collective-permute-start.11) | collective-permute-done | bytes 272416 | tf_op jit(solution)/shard_map/ppermute | solution.py:75
  321.5 5.3 %collective-permute-done.8 = bf16[1,304,448]{2,1,0:T(8,128)(2,1)S(1)} collective-permute-done((bf16[1,304,448]{2,1,0:T(8,128)(2,1)S(1)}, bf16[1,304,448]{2,1,0:T(8,128)(2,1)S(1)}, u32[]{:S(2)}, u32[]{:S(2)}) %collective-permute-start.8) | collective-permute-done | bytes 272416 | tf_op jit(solution)/shard_map/ppermute | solution.py:75
  334.2 5.7 %collective-permute-done = bf16[1,2,2,72,448]{4,3,2,1,0:T(8,128)(2,1)S(1)} collective-permute-done((bf16[1,2,2,72,448]{4,3,2,1,0:T(8,128)(2,1)S(1)}, bf16[1,2,2,72,448]{4,3,2,1,0:T(8,128)(2,1)S(1)}, u32[]{:S(2)}, u32[]{:S(2)}) %collective-permute-start) | collective-permute-done | bytes 258080 | tf_op jit(solution)/shard_map/ppermute | solution.py:75
  341.2 3.4 collective-permute-start.5
  344.6 1.6 collective-permute-done.1
  347.5 1.6 collective-permute-start.2
  351.9 2.0 collective-permute-done.2
  353.9 1.6 fusion.49
  355.5 1.9 fusion.37
  357.3 20.8 %all-reduce.3 = (f32[576]{0:T(1024)}, f32[448]{0:T(512)}, f32[448]{0:T(512)}) all-reduce(f32[576]{0:T(1024)} %reduce_sum.95, f32[448]{0:T(512)} %get-tuple-element.59, f32[448]{0:T(512)} %get-tuple-element.57), channel_id=11, replica_groups=mesh['dp'=8,'tr'=2,'tc'=2] {'dp'}, use_global_device_ids=true, to_apply=%region_22.23.clone | all-reduce | flops 1472 | bytes 11776
  381.9 5.6 %all-reduce.4 = (f32[56]{0:T(128)}, f32[56]{0:T(128)}) all-reduce(f32[56]{0:T(128)} %dynamic-slice.6, f32[56]{0:T(128)} %dynamic-slice.8), channel_id=1, replica_groups=mesh['dp'=8,'tr'=2,'tc'=2] {'tc'}, use_global_device_ids=true, to_apply=%region_24.25 | all-reduce | flops 112 | bytes 896 | tf_op jit(solution)/shard_map/psum | solution.py:285
  387.5 3.2 all-reduce.5
  390.6 2.3 fusion.34
  (205 shorter events, 53.2 us)
Async XLA Ops:
  7.2 48.6 %copy-start = (bf16[448,2432]{1,0:T(8,128)(2,1)S(1)}, bf16[448,2432]{1,0:T(8,128)(2,1)}, u32[]{:S(2)}) copy-start(bf16[448,2432]{1,0:T(8,128)(2,1)} %param.16) | copy-start | bytes 6537220
  7.2 28.6 %reduce-scatter.10.cloned.1.call-start = ((), (), s32[]{:S(2)}) async-start(), calls=%async_computation.9 | async-start | bytes 1769472 | tf_op jit(solution)/shard_map/reduce_scatter | solution.py:68
  8.4 27.4 %copy-start.44 = (f32[576]{0:T(1024)S(1)}, f32[576]{0:T(1024)}, u32[]{:S(2)}) copy-start(f32[576]{0:T(1024)} %param.12) | copy-start | bytes 6916
  22.7 14.3 %copy-start.22 = (bf16[512,448]{0,1:T(8,128)(2,1)}, bf16[512,448]{0,1:T(8,128)(2,1)S(1)}, u32[]{:S(2)}) copy-start(bf16[512,448]{0,1:T(8,128)(2,1)S(1)} %all_gather.27) | copy-start | bytes 1376260
  25.4 40.8 %reduce-scatter.12.cloned.1.call-start = ((), (), s32[]{:S(2)}) async-start(), calls=%async_computation.10 | async-start | bytes 1376256 | tf_op jit(solution)/shard_map/reduce_scatter | solution.py:58
  26.4 13.6 %copy-start.29 = (f32[256,64]{0,1:T(8,128)}, f32[256,64]{0,1:T(8,128)S(1)}, u32[]{:S(2)}) copy-start(f32[256,64]{0,1:T(8,128)S(1)} %get-tuple-element.102) | copy-start | bytes 196612
  39.1 1.6 copy-start.36
  40.0 1.8 copy-start.1
  40.8 1.0 copy-start.42
  40.8 3.9 copy-start.21
  41.9 4.2 %copy-start.19 = (bf16[256,448]{0,1:T(8,128)(2,1)S(1)}, bf16[256,448]{0,1:T(8,128)(2,1)}, u32[]{:S(2)}) copy-start(bf16[256,448]{0,1:T(8,128)(2,1)} %param.17) | copy-start | bytes 688132
  44.7 15.0 %copy-start.11 = (bf16[512,448]{0,1:T(8,128)(2,1)}, bf16[512,448]{0,1:T(8,128)(2,1)S(1)}, u32[]{:S(2)}) copy-start(bf16[512,448]{0,1:T(8,128)(2,1)S(1)} %all_gather.29) | copy-start | bytes 1376260
  46.0 44.5 %reduce-scatter.18.cloned.1.call-start = ((), (), s32[]{:S(2)}) async-start(), calls=%async_computation.14 | async-start | bytes 7471104 | tf_op jit(solution)/shard_map/reduce_scatter | solution.py:68
  59.6 6.6 %copy-start.5 = (bf16[256,448]{0,1:T(8,128)(2,1)S(1)}, bf16[256,448]{0,1:T(8,128)(2,1)}, u32[]{:S(2)}) copy-start(bf16[256,448]{0,1:T(8,128)(2,1)} %param.9) | copy-start | bytes 688132
  59.6 49.9 %reduce-scatter.14.cloned.1.call-start = ((), (), s32[]{:S(2)}) async-start(), calls=%async_computation.11 | async-start | bytes 14942208 | tf_op jit(solution)/shard_map/reduce_scatter | solution.py:68
  90.5 42.6 %all-gather.5.cloned.1.call-start = ((), (), s32[]{:S(2)}) async-start(), calls=%async_computation.15 | async-start | bytes 7471104 | tf_op jit(solution)/shard_map/all_gather | solution.py:64
  116.9 43.6 %reduce-scatter.20.cloned.1.call-start = ((), (), s32[]{:S(2)}) async-start(), calls=%async_computation.16 | async-start | bytes 1376256 | tf_op jit(solution)/shard_map/reduce_scatter | solution.py:58
  140.3 40.2 %all-gather.3.cloned.1.call-start = ((), (), s32[]{:S(2)}) async-start(), calls=%async_computation.12 | async-start | bytes 3735552 | tf_op jit(solution)/shard_map/all_gather | solution.py:64
  141.1 52.3 %reduce-scatter.22.cloned.1.call-start = ((), (), s32[]{:S(2)}) async-start(), calls=%async_computation.17 | async-start | bytes 1376256 | tf_op jit(solution)/shard_map/reduce_scatter | solution.py:68
  166.7 11.9 %copy-start.46 = (u32[32]{0:T(128)S(1)}, u32[32]{0:T(128)}, u32[]{:S(2)}) copy-start(u32[32]{0:T(128)} %constant.246) | copy-start | bytes 388
  175.2 0.8 copy-start.13
  178.5 30.2 %reduce-scatter.24.cloned.1.call-start = ((), (), s32[]{:S(2)}) async-start(), calls=%async_computation.18 | async-start | bytes 393216 | tf_op jit(solution)/shard_map/reduce_scatter | solution.py:68
  191.8 29.0 %collective-permute-start.12 = (bf16[1,2,2,304,448]{4,3,2,1,0:T(8,128)(2,1)}, bf16[1,2,2,304,448]{4,3,2,1,0:T(8,128)(2,1)}, u32[]{:S(2)}, u32[]{:S(2)}) collective-permute-start(bf16[1,2,2,304,448]{4,3,2,1,0:T(8,128)(2,1)} %dynamic-slice_bitcast_fusion), channel_id=1, source_target_pairs={{0,4},{4,0},{8,12},{12,8},{16,20},{20,16},{24,28},{28,24},{1,5},{5... | collective-permute-start | bytes 3268616 | tf_op jit(solution)/shard_map/ppermute | solution.py:75
  194.4 3.2 copy-start.28
  194.4 3.3 copy-start.2
  194.4 3.3 copy-start.37
  194.4 3.3 copy-start.43
  199.1 1.2 copy-start.4
  200.3 1.5 copy-start.30
  200.3 1.5 copy-start.38
  201.7 7.1 %copy-start.39 = (f32[256,1,32]{0,2,1:T(8,128)S(1)}, f32[256,1,32]{0,2,1:T(8,128)}, u32[]{:S(2)}) copy-start(f32[256,1,32]{0,2,1:T(8,128)} %get-tuple-element.103) | copy-start | bytes 98308
  201.7 153.8 %reduce-scatter.26.cloned.1.call-start = ((), (), s32[]{:S(2)}) async-start(), calls=%async_computation.19 | async-start | bytes 1376256 | tf_op jit(solution)/shard_map/reduce_scatter | solution.py:58
  203.8 12.1 %copy-start.9 = (f32[256,1,7,64]{0,3,2,1:T(8,128)}, f32[256,1,7,64]{0,3,2,1:T(8,128)S(1)}, u32[]{:S(2)}) copy-start(f32[256,1,7,64]{0,3,2,1:T(8,128)S(1)} %maximum_subtract_fusion) | copy-start | bytes 1376260
  208.8 5.7 %copy-start.18 = (bf16[448,576]{1,0:T(8,128)(2,1)S(1)}, bf16[448,576]{1,0:T(8,128)(2,1)}, u32[]{:S(2)}) copy-start(bf16[448,576]{1,0:T(8,128)(2,1)} %param.11) | copy-start | bytes 1548292
  216.0 174.7 %reduce-scatter.16.cloned.1.call-start = ((), (), s32[]{:S(2)}) async-start(), calls=%async_computation.13 | async-start | bytes 1376256 | tf_op jit(solution)/shard_map/reduce_scatter | solution.py:58
  216.0 10.3 %copy-start.25 = (bf16[512,448]{0,1:T(8,128)(2,1)S(1)}, bf16[512,448]{0,1:T(8,128)(2,1)}, u32[]{:S(2)}) copy-start(bf16[512,448]{0,1:T(8,128)(2,1)} %copy-done.24) | copy-start | bytes 1376260
  222.8 1.1 copy-start.6
  224.8 30.0 %collective-permute-start.13 = (bf16[1,2,304,448]{3,2,1,0:T(8,128)(2,1)}, bf16[1,2,304,448]{3,2,1,0:T(8,128)(2,1)}, u32[]{:S(2)}, u32[]{:S(2)}) collective-permute-start(bf16[1,2,304,448]{3,2,1,0:T(8,128)(2,1)} %dynamic-slice_bitcast_fusion.2), channel_id=1, source_target_pairs={{0,8},{4,12},{8,0},{12,4},{16,24},{20,28},{24,16},{28,20},{1,9},{5... | collective-permute-start | bytes 1634312 | tf_op jit(solution)/shard_map/ppermute | solution.py:75
  239.2 27.8 %collective-permute-start.9 = (bf16[1,2,2,304,448]{4,3,1,2,0:T(8,128)(2,1)}, bf16[1,2,2,304,448]{4,3,1,2,0:T(8,128)(2,1)}, u32[]{:S(2)}, u32[]{:S(2)}) collective-permute-start(bf16[1,2,2,304,448]{4,3,1,2,0:T(8,128)(2,1)} %bitcast.284), channel_id=1, source_target_pairs={{0,4},{4,0},{8,12},{12,8},{16,20},{20,16},{24,28},{28,24},{1,5},{5... | collective-permute-start | bytes 3268616 | tf_op jit(solution)/shard_map/ppermute | solution.py:75
  249.4 3.1 copy-start.45
  252.0 37.3 %collective-permute-start.6 = (bf16[1,2,2,304,448]{4,3,2,1,0:T(8,128)(2,1)}, bf16[1,2,2,304,448]{4,3,2,1,0:T(8,128)(2,1)}, u32[]{:S(2)}, u32[]{:S(2)}) collective-permute-start(bf16[1,2,2,304,448]{4,3,2,1,0:T(8,128)(2,1)} %dynamic-slice_bitcast_fusion.1), channel_id=1, source_target_pairs={{0,8},{4,12},{8,0},{12,4},{16,24},{20,28},{24,16},{28,20},{1,9},{5... | collective-permute-start | bytes 3268616 | tf_op jit(solution)/shard_map/ppermute | solution.py:75
  254.8 12.2 %copy-start.7 = (bf16[1,2,2,1,304,448]{5,4,3,2,1,0:T(8,128)(2,1)S(1)}, bf16[1,2,2,1,304,448]{5,4,3,2,1,0:T(8,128)(2,1)}, u32[]{:S(2)}) copy-start(bf16[1,2,2,1,304,448]{5,4,3,2,1,0:T(8,128)(2,1)} %get-tuple-element.85) | copy-start | bytes 3268612
  256.4 35.2 %collective-permute-start.14 = (bf16[1,304,448]{2,1,0:T(8,128)(2,1)S(1)}, bf16[1,304,448]{2,1,0:T(8,128)(2,1)S(1)}, u32[]{:S(2)}, u32[]{:S(2)}) collective-permute-start(bf16[1,304,448]{2,1,0:T(8,128)(2,1)S(1)} %dynamic-slice_bitcast_fusion.5), channel_id=1, source_target_pairs={{0,16},{4,20},{8,24},{12,28},{16,0},{20,4},{24,8},{28,12},{1,17},{... | collective-permute-start | bytes 817160 | tf_op jit(solution)/shard_map/ppermute | solution.py:75
  267.0 22.3 %copy-start.3 = (bf16[2432,448]{1,0:T(8,128)(2,1)S(1)}, bf16[2432,448]{1,0:T(8,128)(2,1)}, u32[]{:S(2)}) copy-start(bf16[2432,448]{1,0:T(8,128)(2,1)} %copy.51) | copy-start | bytes 6537220
  268.8 30.6 %collective-permute-start.10 = (bf16[1,2,304,448]{3,2,1,0:T(8,128)(2,1)S(1)}, bf16[1,2,304,448]{3,2,1,0:T(8,128)(2,1)S(1)}, u32[]{:S(2)}, u32[]{:S(2)}) collective-permute-start(bf16[1,2,304,448]{3,2,1,0:T(8,128)(2,1)S(1)} %dynamic-slice_bitcast_fusion.3), channel_id=1, source_target_pairs={{0,8},{4,12},{8,0},{12,4},{16,24},{20,28},{24,16},{28,20},{1,9},{5... | collective-permute-start | bytes 1634312 | tf_op jit(solution)/shard_map/ppermute | solution.py:75
  291.0 12.0 %collective-permute-start.7 = (bf16[1,2,304,448]{3,2,1,0:T(8,128)(2,1)S(1)}, bf16[1,2,304,448]{3,2,1,0:T(8,128)(2,1)S(1)}, u32[]{:S(2)}, u32[]{:S(2)}) collective-permute-start(bf16[1,2,304,448]{3,2,1,0:T(8,128)(2,1)S(1)} %dynamic-slice_bitcast_fusion.4), channel_id=1, source_target_pairs={{0,4},{4,0},{8,12},{12,8},{16,20},{20,16},{24,28},{28,24},{1,5},{5... | collective-permute-start | bytes 1634312 | tf_op jit(solution)/shard_map/ppermute | solution.py:75
  292.5 10.7 %copy-start.12 = (bf16[512,448]{0,1:T(8,128)(2,1)S(1)}, bf16[512,448]{0,1:T(8,128)(2,1)}, u32[]{:S(2)}) copy-start(bf16[512,448]{0,1:T(8,128)(2,1)} %copy-done.11) | copy-start | bytes 1376260
  292.5 10.7 %copy-start.14 = (bf16[512,448]{0,1:T(8,128)(2,1)S(1)}, bf16[512,448]{0,1:T(8,128)(2,1)}, u32[]{:S(2)}) copy-start(bf16[512,448]{0,1:T(8,128)(2,1)} %copy-done.13) | copy-start | bytes 1376260
  299.6 21.8 %collective-permute-start.11 = (bf16[1,304,448]{2,1,0:T(8,128)(2,1)S(1)}, bf16[1,304,448]{2,1,0:T(8,128)(2,1)S(1)}, u32[]{:S(2)}, u32[]{:S(2)}) collective-permute-start(bf16[1,304,448]{2,1,0:T(8,128)(2,1)S(1)} %dynamic-slice_bitcast_fusion.6), channel_id=1, source_target_pairs={{0,16},{4,20},{8,24},{12,28},{16,0},{20,4},{24,8},{28,12},{1,17},{... | collective-permute-start | bytes 817160 | tf_op jit(solution)/shard_map/ppermute | solution.py:75
  303.2 23.6 %collective-permute-start.8 = (bf16[1,304,448]{2,1,0:T(8,128)(2,1)S(1)}, bf16[1,304,448]{2,1,0:T(8,128)(2,1)S(1)}, u32[]{:S(2)}, u32[]{:S(2)}) collective-permute-start(bf16[1,304,448]{2,1,0:T(8,128)(2,1)S(1)} %dynamic-slice_bitcast_fusion.7), channel_id=1, source_target_pairs={{0,16},{4,20},{8,24},{12,28},{16,0},{20,4},{24,8},{28,12},{1,17},{... | collective-permute-start | bytes 817160 | tf_op jit(solution)/shard_map/ppermute | solution.py:75
  305.2 22.9 %copy-start.17 = (bf16[512,576]{0,1:T(8,128)(2,1)S(1)}, bf16[512,576]{0,1:T(8,128)(2,1)}, u32[]{:S(2)}) copy-start(bf16[512,576]{0,1:T(8,128)(2,1)} %copy-done.16) | copy-start | bytes 1769476
  305.2 22.9 %copy-start.23 = (bf16[512,448]{0,1:T(8,128)(2,1)S(1)}, bf16[512,448]{0,1:T(8,128)(2,1)}, u32[]{:S(2)}) copy-start(bf16[512,448]{0,1:T(8,128)(2,1)} %copy-done.22) | copy-start | bytes 1376260
  305.2 26.3 %collective-permute-start.3 = (bf16[1,2,2,56,448]{4,3,1,2,0:T(8,128)(2,1)}, bf16[1,2,2,56,448]{4,3,1,2,0:T(8,128)(2,1)}, u32[]{:S(2)}, u32[]{:S(2)}) collective-permute-start(bf16[1,2,2,56,448]{4,3,1,2,0:T(8,128)(2,1)} %bitcast.285), channel_id=1, source_target_pairs={{0,8},{4,12},{8,0},{12,4},{16,24},{20,28},{24,16},{28,20},{1,9},{5... | collective-permute-start | bytes 602120 | tf_op jit(solution)/shard_map/ppermute | solution.py:75
  330.8 0.8 copy-start.15
  330.8 19.0 %copy-start.10 = (f32[256,1,7,64]{0,3,2,1:T(8,128)S(1)}, f32[256,1,7,64]{0,3,2,1:T(8,128)}, u32[]{:S(2)}) copy-start(f32[256,1,7,64]{0,3,2,1:T(8,128)} %copy-done.9) | copy-start | bytes 1376260
  330.8 19.0 %copy-start.32 = (f32[256,1,1,64]{0,3,2,1:T(8,128)S(1)}, f32[256,1,1,64]{0,3,2,1:T(8,128)}, u32[]{:S(2)}) copy-start(f32[256,1,1,64]{0,3,2,1:T(8,128)} %copy-done.31) | copy-start | bytes 196612
  330.8 19.0 %copy-start.34 = (f32[256,1,1,64]{0,3,2,1:T(8,128)S(1)}, f32[256,1,1,64]{0,3,2,1:T(8,128)}, u32[]{:S(2)}) copy-start(f32[256,1,1,64]{0,3,2,1:T(8,128)} %copy-done.33) | copy-start | bytes 196612
  330.8 9.0 %collective-permute-start = (bf16[1,2,2,72,448]{4,3,2,1,0:T(8,128)(2,1)S(1)}, bf16[1,2,2,72,448]{4,3,2,1,0:T(8,128)(2,1)S(1)}, u32[]{:S(2)}, u32[]{:S(2)}) collective-permute-start(bf16[1,2,2,72,448]{4,3,2,1,0:T(8,128)(2,1)S(1)} %dynamic-slice_bitcast_fusion.8), channel_id=1, source_target_pairs={{0,4},{4,0},{8,12},{12,8},{16,20},{20,16},{24,28},{28,24},{1,5},{5... | collective-permute-start | bytes 774152 | tf_op jit(solution)/shard_map/ppermute | solution.py:75
  331.6 59.0 %copy-start.8 = (f32[256,448]{0,1:T(8,128)S(1)}, f32[256,448]{0,1:T(8,128)}, u32[]{:S(2)}) copy-start(f32[256,448]{0,1:T(8,128)} %reduce-scatter.20.cloned.1.call-done) | copy-start | bytes 1376260
  331.6 59.0 %copy-start.20 = (bf16[256,448]{0,1:T(8,128)(2,1)S(1)}, bf16[256,448]{0,1:T(8,128)(2,1)}, u32[]{:S(2)}) copy-start(bf16[256,448]{0,1:T(8,128)(2,1)} %param.17) | copy-start | bytes 688132
  332.8 8.3 %collective-permute-start.4 = (bf16[1,2,56,448]{3,2,1,0:T(8,128)(2,1)S(1)}, bf16[1,2,56,448]{3,2,1,0:T(8,128)(2,1)S(1)}, u32[]{:S(2)}, u32[]{:S(2)}) collective-permute-start(bf16[1,2,56,448]{3,2,1,0:T(8,128)(2,1)S(1)} %dynamic-slice_bitcast_fusion.10), channel_id=1, source_target_pairs={{0,4},{4,0},{8,12},{12,8},{16,20},{20,16},{24,28},{28,24},{1,5},{5... | collective-permute-start | bytes 301064 | tf_op jit(solution)/shard_map/ppermute | solution.py:75
  341.0 5.2 %collective-permute-start.1 = (bf16[1,2,72,448]{3,2,1,0:T(8,128)(2,1)S(1)}, bf16[1,2,72,448]{3,2,1,0:T(8,128)(2,1)S(1)}, u32[]{:S(2)}, u32[]{:S(2)}) collective-permute-start(bf16[1,2,72,448]{3,2,1,0:T(8,128)(2,1)S(1)} %dynamic-slice_bitcast_fusion.9), channel_id=1, source_target_pairs={{0,8},{4,12},{8,0},{12,4},{16,24},{20,28},{24,16},{28,20},{1,9},{5... | collective-permute-start | bytes 387080 | tf_op jit(solution)/shard_map/ppermute | solution.py:75
  341.2 8.0 %collective-permute-start.5 = (bf16[1,56,448]{2,1,0:T(8,128)(2,1)S(1)}, bf16[1,56,448]{2,1,0:T(8,128)(2,1)S(1)}, u32[]{:S(2)}, u32[]{:S(2)}) collective-permute-start(bf16[1,56,448]{2,1,0:T(8,128)(2,1)S(1)} %dynamic-slice_bitcast_fusion.12), channel_id=1, source_target_pairs={{0,16},{4,20},{8,24},{12,28},{16,0},{20,4},{24,8},{28,12},{1,17},{... | collective-permute-start | bytes 150536 | tf_op jit(solution)/shard_map/ppermute | solution.py:75
  347.5 6.4 %collective-permute-start.2 = (bf16[1,72,448]{2,1,0:T(8,128)(2,1)}, bf16[1,72,448]{2,1,0:T(8,128)(2,1)}, u32[]{:S(2)}, u32[]{:S(2)}) collective-permute-start(bf16[1,72,448]{2,1,0:T(8,128)(2,1)} %dynamic-slice_bitcast_fusion.11), channel_id=1, source_target_pairs={{0,16},{4,20},{8,24},{12,28},{16,0},{20,4},{24,8},{28,12},{1,17},{... | collective-permute-start | bytes 193544 | tf_op jit(solution)/shard_map/ppermute | solution.py:75
  (9 other events, 6.1 us)
Sparse Core Ops, SparseCore 0:
  25.6 10.1 reduce-scatter.9
  46.1 20.0 reduce-scatter.11
  68.6 13.3 reduce-scatter.17
  90.6 18.8 reduce-scatter.13
  117.0 16.0 all-gather.4
  140.4 20.0 reduce-scatter.19
  162.6 11.1 all-gather.2
  178.6 8.4 reduce-scatter.21
  201.8 6.9 reduce-scatter.23
  216.1 20.0 reduce-scatter.25
  254.9 18.0 reduce-scatter.15
